TPU v7x, 32 devices: a whole 2x2x4 slice. The times are simulated.
32 devices in a mesh: alpha: 4 (over y, x), beta: 8 (over z, core).
Axes of the slice: x: 2, y: 2, z: 4, core: 2. Of those that a mesh axis runs over, the one named last changes fastest.
Arguments:
- coefficients: bfloat16 [1024, 2048], P('alpha', 'beta'), may hold values from -6 to 6
- diagonal: float32 [1024, 2048], P('alpha', 'beta'), may hold values from 0.3 to 3
- integrals: bfloat16 [324, 324], replicated, may hold values from -0.02734375 to 0.02734375
- alpha_row: int32 [324, 1024], replicated, may hold values from 0 to 1023
- alpha_sign: int32 [324, 1024], replicated, may hold values from -1 to 1
- beta_block: int32 [32, 324], P('beta'), may hold values from 0 to 31
- beta_sign: int32 [32, 20736], P('beta'), may hold values from -1 to 1
- block_irrep: int32 [16], replicated, may hold values from 0 to 7, as said below
Outputs:
- sigma: float32 [1024, 2048], P('alpha', 'beta')
Inputs may be any that keep to these rules, and one draw needn't show every extreme that they name: `block_irrep`: irrep 0 is the window's. The 4 blocks held by one index of alpha include 1 to 4 blocks of irrep 0, and some index holds 4 of them.
All inputs are finite; a program needn't handle non-finite values.
Results may differ from a plain program's by a relative error of at most 0.0003.
Values may be sent and summed in bfloat16 or wider, within the bound.
No kernel may reach another device: no remote copies, remote signals or barrier semaphores. Data moves between devices by JAX's collectives and lax.ppermute only.
A program may use at most 128 MiB of HBM per device.

v0:
```python
import functools

import jax
import jax.numpy as jnp
from jax import lax
from jax.experimental import pallas as pl
from jax.experimental.pallas import tpu as pltpu
from jax.sharding import PartitionSpec as P

LANES = 128
DEPTH = 512
SPAN = 256
GATHERED = 4
VMEM = pl.BlockSpec(memory_space=pltpu.VMEM)
SMEM = pl.BlockSpec(memory_space=pltpu.SMEM)


def round_up(size, step):
    return -(-size // step) * step


class Sizes:
    def __init__(self, coefficients, integrals, alpha_row, beta_sign, block_irrep):
        self.n_alpha = lax.axis_size("alpha")
        self.n_beta = lax.axis_size("beta")
        self.devices = self.n_alpha * self.n_beta
        self.rows, self.cols = coefficients.shape
        self.pairs = integrals.shape[0]
        self.block = beta_sign.shape[1] // self.pairs
        self.src = self.cols // self.block
        self.targets = self.n_beta * self.src
        self.all_rows = alpha_row.shape[1]
        self.blocks = block_irrep.shape[0]
        self.own = self.rows // self.block
        self.share = max(1, self.devices // self.block)
        self.sets = self.devices // self.share
        self.strings = self.block // self.sets
        self.halves = self.rows // LANES
        self.tiles = self.all_rows // LANES
        self.per = max(1, self.src // self.n_alpha)
        self.senders = self.src // self.per
        self.group = self.src * self.strings
        self.lists = self.n_beta * self.group
        self.chunk_pairs = DEPTH // self.targets
        self.pair_rows = round_up(self.pairs, self.chunk_pairs)
        self.chunks = self.pair_rows // self.chunk_pairs
        self.pair_lanes = round_up(self.pairs, LANES)
        self.pair_tiles = self.pair_lanes // LANES
        self.coef_rows = self.halves * self.group
        self.sign_rows = self.per * self.strings * self.pair_tiles
        self.pack = round_up(self.coef_rows + self.sign_rows, 8)


def pack_kernel(z, coef_ref, sign_ref, out_ref, scratch):
    scratch[...] = jnp.zeros_like(scratch)
    turned = coef_ref[...].astype(jnp.float32).T
    for half in range(z.halves):
        for g in range(z.group):
            row = half * z.group + g
            for part in range(z.share):
                scratch[pl.ds(row + part * z.pack, z.sets, stride=z.share * z.pack), :] = turned[
                    g * z.sets : (g + 1) * z.sets, half * LANES : (half + 1) * LANES
                ]
    for s in range(z.per):
        code = sign_ref[s].T
        code = jnp.concatenate(
            [code, jnp.zeros((z.block, z.pair_lanes - z.pairs), jnp.float32)], axis=1
        )
        for cc in range(z.strings):
            for k in range(z.pair_tiles):
                row = z.coef_rows + (s * z.strings + cc) * z.pair_tiles + k
                for part in range(z.share):
                    scratch[pl.ds(row + part * z.pack, z.sets, stride=z.share * z.pack), :] = code[
                        cc * z.sets : (cc + 1) * z.sets, k * LANES : (k + 1) * LANES
                    ]
    out_ref[...] = scratch[...].astype(jnp.bfloat16)


def live_blocks(z, irrep_ref, rank_ref, list_ref):
    count = jnp.int32(0)
    lane_row = lax.broadcasted_iota(jnp.int32, (1, LANES), 1)
    ranks = jnp.full((1, LANES), -1, jnp.int32)
    for g in range(z.blocks):
        live = irrep_ref[g] == 0
        rank = jnp.where(live, count, -1)
        rank_ref[g] = rank
        list_ref[count] = g
        ranks = jnp.where(lane_row == g, rank, ranks)
        count = count + live.astype(jnp.int32)
    for extra in range(4):
        list_ref[count + extra] = 0
    return count, ranks


def index_kernel(z, irrep_ref, row_ref, sign_ref, out_ref, rank_ref, list_ref):
    count, ranks = live_blocks(z, irrep_ref, rank_ref, list_ref)
    lane_pair = lax.broadcasted_iota(jnp.int32, (z.pairs, LANES), 1)
    tail = z.pairs // 8 * 8

    def compact_step(u, carry):
        first, second = list_ref[2 * u], list_ref[2 * u + 1]
        left_shift = (first % 2) * z.block
        right_shift = (1 - second % 2) * z.block

        def merged(ref):
            at_first = pl.ds(pl.multiple_of(first // 2 * LANES, LANES), LANES)
            at_second = pl.ds(pl.multiple_of(second // 2 * LANES, LANES), LANES)
            return jnp.where(
                lane_pair < z.block,
                pltpu.roll(ref[:, at_first], left_shift, 1),
                pltpu.roll(ref[:, at_second], right_shift, 1),
            )

        source = merged(row_ref)
        signs = merged(sign_ref)
        block = source // z.block
        rank = jnp.take_along_axis(
            jnp.broadcast_to(ranks, (z.pairs, LANES)), block, axis=1, mode="promise_in_bounds"
        )
        spot = rank * z.block + (source & (z.block - 1))
        inside = (lane_pair < z.block) | (2 * u + 1 < count)
        out_ref[u, tail : z.pair_rows, :] = jnp.zeros((z.pair_rows - tail, LANES), jnp.int32)
        out_ref[u, 0 : z.pairs, :] = jnp.where((rank >= 0) & inside, signs * (spot + 1), 0)
        return carry

    lax.fori_loop(0, (count + 1) // 2, compact_step, 0)


def main_kernel(
    z,
    irrep_ref,
    part_ref,
    rx_ref,
    integ_ref,
    spot_ref,
    out_ref,
    rxf,
    full,
    tabf,
    table,
    codes,
    tall,
    weights,
    acc,
    held,
    result,
    rank_ref,
    list_ref,
):
    f32, bf16 = jnp.float32, jnp.bfloat16
    half_block = z.block
    count, _ = live_blocks(z, irrep_ref, rank_ref, list_ref)
    n_tiles = (count + 1) // 2

    rxf[...] = rx_ref[...].astype(f32)
    for i in range(z.n_alpha):
        base = i * z.n_beta * z.pack
        for half in range(z.halves):
            for s in range(z.src):
                for cc in range(z.strings):
                    source = base + half * z.group + s * z.strings + cc
                    dest = cc * z.targets + s
                    full[i * z.halves + half, pl.ds(dest, z.n_beta, stride=z.src), :] = rxf[
                        pl.ds(source, z.n_beta, stride=z.pack), :
                    ]
        for s in range(z.per if i < z.senders else 0):
            for cc in range(z.strings):
                for k in range(z.pair_tiles):
                    source = base + z.coef_rows + (s * z.strings + cc) * z.pair_tiles + k
                    dest = (i * z.per + s) * z.strings + cc
                    codes[k, pl.ds(dest, z.n_beta, stride=z.group), :] = rxf[
                        pl.ds(source, z.n_beta, stride=z.pack), :
                    ]

    step = 4
    target = (lax.broadcasted_iota(jnp.int32, (z.targets, z.pair_lanes), 0) + 1).astype(f32)

    def weight_step(n, carry):
        parts = []
        for m in range(step * z.strings):
            code = jnp.concatenate(
                [codes[k, pl.ds(n * step * z.strings + m, 1), :] for k in range(z.pair_tiles)],
                axis=1,
            )
            hit = jnp.where(code == target, 1.0, 0.0) - jnp.where(code == -target, 1.0, 0.0)
            parts.append(hit)
        hits = jnp.concatenate(parts, axis=0).astype(bf16)
        found = jnp.dot(hits, integ_ref[...], preferred_element_type=f32)
        high = found.astype(bf16).astype(f32)
        low = found - high
        for m in range(step):
            rows = []
            for cc in range(z.strings):
                at = (m * z.strings + cc) * z.targets
                rows += [high[at : at + z.targets], low[at : at + z.targets]]
            turned = jnp.concatenate(rows, axis=0).T
            tall[pl.ds(n * step + m, z.pair_rows, stride=z.targets), :] = turned[0 : z.pair_rows]
        return carry

    lax.fori_loop(0, z.targets // step, weight_step, 0, unroll=2)

    lane_list = lax.broadcasted_iota(jnp.int32, (z.lists, LANES), 1)
    chunk_tiles = SPAN // LANES

    def compact_step(u, carry):
        first, second = list_ref[2 * u], list_ref[2 * u + 1]
        left_shift = (first % 2) * half_block
        right_shift = (1 - second % 2) * half_block
        left = pltpu.roll(full[first // 2], left_shift, 1)
        right = pltpu.roll(full[second // 2], right_shift, 1)
        left = jnp.where(2 * u < count, left, 0.0)
        right = jnp.where(2 * u + 1 < count, right, 0.0)
        at_list = pl.ds(pl.multiple_of(u // chunk_tiles * z.lists, z.lists), z.lists)
        at_lane = pl.ds(pl.multiple_of(u % chunk_tiles * LANES, LANES), LANES)
        both = jnp.where(lane_list < half_block, left, right)
        tabf[u] = both
        table[at_list, at_lane] = both.astype(bf16)
        return carry

    lax.fori_loop(0, (n_tiles + chunk_tiles - 1) // chunk_tiles * chunk_tiles, compact_step, 0)

    local = lax.broadcasted_iota(jnp.int32, (SPAN, LANES), 0).astype(f32).astype(bf16)
    nothing = jnp.zeros((SPAN, LANES), bf16)
    side = 2 * z.targets

    def tall_row(few):
        return jnp.concatenate([few.astype(f32).astype(bf16)] * (SPAN // 16), axis=0)

    def run(tiles):
        depth = (tiles * LANES + SPAN - 1) // SPAN

        def one_tile(u, carry, turn=False):
            acc[...] = jnp.zeros_like(acc)
            held[...] = jnp.zeros_like(held)

            def spread(n):
                if turn:
                    at = pl.multiple_of(n * DEPTH, DEPTH)
                    turned = tall[pl.ds(at, DEPTH), :].T.astype(bf16)
                    weights[n] = turned
                else:
                    turned = weights[n]
                total = jnp.dot(turned, held[...], preferred_element_type=f32)
                for cc in range(z.strings):
                    acc[cc] += total[
                        cc * side : (cc + 1) * side, cc * LANES : (cc + 1) * LANES
                    ]

            def keep(q, value):
                value = value.astype(bf16)
                for cc in range(z.strings):
                    held[q * z.targets : (q + 1) * z.targets, cc * LANES : (cc + 1) * LANES] = (
                        value[cc * z.targets : (cc + 1) * z.targets]
                    )

            def gather(q, spot, sign):
                lanes = spot & (LANES - 1)
                tile = lax.shift_right_arithmetic(spot, LANES.bit_length() - 1)
                hits = [tile == k for k in range(tiles)]
                parts = []
                for row in range(0, z.lists, 8):
                    value = jnp.zeros((8, LANES), f32)
                    for k in range(tiles):
                        taken = jnp.take_along_axis(
                            tabf[k, row : row + 8, :], lanes, axis=1, mode="promise_in_bounds"
                        )
                        value = jnp.where(hits[k], taken, value)
                    parts.append(value * sign)
                keep(q, jnp.concatenate(parts, axis=0))

            def one_chunk(n, inner):
                spread(jnp.maximum(n - 1, 0))
                picks, chunk, chosen = [], [], []
                for q in range(z.chunk_pairs):
                    at = pl.ds(n * z.chunk_pairs + q, 1)
                    code = jnp.broadcast_to(spot_ref[u, at, :], (16, LANES))
                    spot = jnp.abs(code) - 1
                    sign = jnp.clip(code, -1, 1)
                    if q % GATHERED == GATHERED - 1:
                        gather(q, spot[0:8], sign[0:8].astype(f32))
                        continue
                    chosen.append(q)
                    hit = local == tall_row(spot & (SPAN - 1))
                    picks.append(jnp.where(hit, tall_row(sign), nothing))
                    chunk.append(lax.shift_right_arithmetic(spot[0:8], SPAN.bit_length() - 1))
                pick = jnp.concatenate(picks, axis=1)
                found = jnp.dot(
                    table[0 : depth * z.lists, :], pick, preferred_element_type=f32
                )
                for k, q in enumerate(chosen):
                    lanes = slice(k * LANES, (k + 1) * LANES)
                    value = found[0 : z.lists, lanes]
                    for m in range(1, depth):
                        other = found[m * z.lists : (m + 1) * z.lists, lanes]
                        here = jnp.concatenate([chunk[k] == m] * (z.lists // 8), axis=0)
                        value = jnp.where(here, other, value)
                    keep(q, value)
                return inner

            lax.fori_loop(0, z.chunks, one_chunk, 0)
            spread(z.chunks - 1)
            for cc in range(z.strings):
                total = acc[cc, 0 : z.targets, :] + acc[cc, z.targets : 2 * z.targets, :]
                result[u, pl.ds(cc, z.targets, stride=z.strings), :] = total
            return carry

        if z.share == 1:
            one_tile(0, 0, turn=True)
            lax.fori_loop(1, n_tiles, one_tile, 0)
        else:
            part = part_ref[0]
            mine = (n_tiles - part + z.share - 1) // z.share
            lax.fori_loop(0, mine, lambda n, carry: one_tile(n * z.share + part, carry, True), 0)

    lower = 0
    for tiles in sorted({min(tiles, z.tiles) for tiles in (4, 5, 6, 8, z.tiles)}):
        pl.when((n_tiles > lower) & (n_tiles <= tiles))(functools.partial(run, tiles))
        lower = tiles

    wide = z.src * z.strings
    lane_out = lax.broadcasted_iota(jnp.int32, (z.targets * z.strings, LANES), 1)
    for w in range(z.tiles):
        sides = []
        for at_side in range(2):
            rank = rank_ref[2 * w + at_side]
            spot = jnp.maximum(rank, 0)
            shift = ((spot + at_side) % 2) * half_block
            moved = pltpu.roll(result[spot // 2], shift, 1)
            here = rank >= 0
            if z.share > 1:
                here = here & ((spot // 2) % z.share == part_ref[0])
            sides.append(jnp.where(here, moved, 0.0))
        both = jnp.where(lane_out < half_block, sides[0], sides[1])
        for j in range(z.n_beta):
            device = w // z.halves * z.n_beta + j
            out_ref[device, w % z.halves] = both[j * wide : (j + 1) * wide]


def finish_kernel(z, irrep_ref, rx_ref, diag_ref, coef_ref, out_ref):
    wide = z.src * z.strings
    stride = z.share * z.halves * wide

    def column(first):
        rows = [
            rx_ref[pl.ds(part * z.halves * wide + first, z.sets, stride=stride), :]
            for part in range(z.share)
        ]
        return functools.reduce(jnp.add, rows)

    columns = []
    for t in range(z.src):
        for cc in range(z.strings):
            firsts = [h * wide + t * z.strings + cc for h in range(z.halves)]
            columns.append(jnp.concatenate([column(first) for first in firsts], axis=1))
    added = jnp.concatenate(columns, axis=0).T
    total = diag_ref[...] * coef_ref[...].astype(jnp.float32) + added
    for b in range(z.own):
        at = slice(b * z.block, (b + 1) * z.block)
        out_ref[at, :] = jnp.where(irrep_ref[b] == 0, total[at], 0.0)


def on_device(
    coefficients, diagonal, integrals, alpha_row, alpha_sign, beta_block, beta_sign, block_irrep
):
    z = Sizes(coefficients, integrals, alpha_row, beta_sign, block_irrep)
    f32, i32, bf16 = jnp.float32, jnp.int32, jnp.bfloat16
    alpha_rank = lax.axis_index("alpha")
    params = pltpu.CompilerParams(vmem_limit_bytes=32 * 1024 * 1024)

    first = jnp.minimum(alpha_rank, z.senders - 1) * z.per
    own_signs = lax.dynamic_slice_in_dim(beta_sign, first, z.per, 0)
    own_blocks = lax.dynamic_slice_in_dim(beta_block, first, z.per, 0)
    code = own_signs.reshape(z.per, z.pairs, z.block) * (own_blocks + 1)[:, :, None]
    packed = pl.pallas_call(
        functools.partial(pack_kernel, z),
        out_shape=jax.ShapeDtypeStruct((z.devices * z.pack, LANES), bf16),
        in_specs=[VMEM, VMEM],
        out_specs=VMEM,
        scratch_shapes=[pltpu.VMEM((z.devices * z.pack, LANES), f32)],
        compiler_params=params,
    )(coefficients, code.astype(f32))
    arrived = lax.all_to_all(
        packed.reshape(z.devices, z.pack, LANES), ("alpha", "beta"), 0, 0, tiled=True
    ).reshape(z.devices * z.pack, LANES)

    pad = z.pair_lanes - z.pairs
    wide = z.src * z.strings
    part = (alpha_rank * z.n_beta + lax.axis_index("beta")) % z.share
    integ = jnp.pad(integrals, ((0, pad), (0, pad)))
    lists = [pltpu.SMEM((z.blocks,), i32), pltpu.SMEM((z.blocks + 8,), i32)]
    spots = pl.pallas_call(
        functools.partial(index_kernel, z),
        out_shape=jax.ShapeDtypeStruct((z.tiles, z.pair_rows, LANES), i32),
        in_specs=[SMEM, VMEM, VMEM],
        out_specs=VMEM,
        scratch_shapes=lists,
        compiler_params=pltpu.CompilerParams(vmem_limit_bytes=16 * 1024 * 1024),
        cost_estimate=pl.CostEstimate(
            flops=50 * z.pairs * z.all_rows,
            bytes_accessed=12 * z.pairs * z.all_rows,
            transcendentals=0,
        ),
    )(block_irrep, alpha_row, alpha_sign)
    terms = pl.pallas_call(
        functools.partial(main_kernel, z),
        out_shape=jax.ShapeDtypeStruct((z.devices, z.halves, wide, LANES), f32),
        in_specs=[SMEM, SMEM, VMEM, VMEM, VMEM],
        out_specs=VMEM,
        scratch_shapes=[
            pltpu.VMEM((z.devices * z.pack, LANES), f32),
            pltpu.VMEM((z.tiles, z.lists, LANES), f32),
            pltpu.VMEM((z.tiles, z.lists, LANES), f32),
            pltpu.VMEM((z.tiles * LANES // SPAN * z.lists, SPAN), bf16),
            pltpu.VMEM((z.pair_tiles, z.lists, LANES), f32),
            pltpu.VMEM((z.pair_rows * z.targets, LANES), f32),
            pltpu.VMEM((z.chunks, LANES, DEPTH), bf16),
            pltpu.VMEM((z.strings, 2 * z.targets, LANES), f32),
            pltpu.VMEM((DEPTH, z.strings * LANES), bf16),
            pltpu.VMEM((z.tiles, z.targets * z.strings, LANES), f32),
        ]
        + lists,
        compiler_params=params,
    )(block_irrep, part.astype(i32)[None], arrived, integ, spots)

    back = lax.all_to_all(terms, ("alpha", "beta"), 0, 0, tiled=True).reshape(-1, LANES)
    own_irrep = lax.dynamic_slice_in_dim(block_irrep, alpha_rank * z.own, z.own, 0)
    return pl.pallas_call(
        functools.partial(finish_kernel, z),
        out_shape=jax.ShapeDtypeStruct((z.rows, z.cols), f32),
        in_specs=[SMEM, VMEM, VMEM, VMEM],
        out_specs=VMEM,
        compiler_params=params,
    )(own_irrep, back, diagonal, coefficients)


def solution(mesh):
    return jax.shard_map(
        on_device,
        mesh=mesh,
        in_specs=(
            P("alpha", "beta"),
            P("alpha", "beta"),
            P(),
            P(),
            P(),
            P("beta", None),
            P("beta", None),
            P(),
        ),
        out_specs=P("alpha", "beta"),
        check_vma=False,
    )
```

profile of v0, /device:TPU:0, one launch (start us, length us, event | category | flops | bytes accessed | tf_op | source)
XLA Modules:
  0.0 82.3 jit_solution(14906946067463328274)
XLA Ops:
  0.0 0.0 copy-start
  0.0 0.0 copy-start.1
  0.0 0.8 %add_reduce_fusion = s32[324]{0:T(512)S(1)} fusion(s32[4,324]{1,0:T(4,128)} %param.13, s32[]{:T(128)S(6)} %select_n.13), kind=kLoop, calls=%fused_computation.2 | loop fusion | flops 324 | bytes 2596 | tf_op jit(solution)/shard_map/add | solution.py:373
  0.8 0.1 copy-done
  1.0 0.2 dynamic-slice_reduce_fusion
  1.2 0.1 reshape.55
  1.3 0.1 multiply_convert_fusion.sign_ref
  1.4 0.0 copy-start.3
  1.4 0.9 %copy-done.3 = bf16[256,256]{1,0:T(8,128)(2,1)S(1)} copy-done((bf16[256,256]{1,0:T(8,128)(2,1)S(1)}, bf16[256,256]{1,0:T(8,128)(2,1)}, u32[]{:S(2)}) %copy-start.3) | copy-done | bytes 131096
  2.3 0.0 copy-start.6
  2.3 0.8 %shard_map.82 = bf16[768,128]{1,0:T(8,128)(2,1)} custom-call(bf16[256,256]{1,0:T(8,128)(2,1)S(1)} %copy-done.3, f32[1,324,64]{2,1,0:T(8,128)S(1)} %multiply_convert_fusion.sign_ref), custom_call_target="tpu_custom_call" | custom-call | tf_op jit(solution)/shard_map/pallas_call | solution.py:374
  3.2 7.3 %all-to-all-start = ((bf16[32,24,128]{2,1,0:T(8,128)(2,1)}), bf16[32,24,128]{2,1,0:T(8,128)(2,1)S(1)}, u32[]{:S(2)}, u32[]{:S(2)}) async-start(bf16[32,24,128]{2,1,0:T(8,128)(2,1)} %bitcast), calls=%async_computation | async-start | bytes 393216 | tf_op jit(solution)/shard_map/all_to_all | solution.py:382
  10.5 1.0 %pad.4.integ_ref = bf16[384,384]{1,0:T(8,128)(2,1)S(1)} pad(bf16[324,324]{1,0:T(8,128)(2,1)} %param.10, bf16[]{:T(256)} %constant.32.clone.1), padding=0_60x0_60 | pad | bytes 504866 | tf_op jit(solution)/shard_map/jit(_pad)/pad | solution.py:389
  11.5 0.0 copy-done.1
  11.5 0.0 copy-done.6
  11.5 0.0 copy-start.2
  11.5 1.3 %copy-done.2 = s32[324,1024]{1,0:T(8,128)S(1)} copy-done((s32[324,1024]{1,0:T(8,128)S(1)}, s32[324,1024]{1,0:T(8,128)}, u32[]{:S(2)}) %copy-start.2) | copy-done | bytes 1327128
  12.8 2.5 %shard_map.83.spot_ref = s32[8,336,128]{2,1,0:T(8,128)S(1)} custom-call(s32[16]{0:T(128)S(1)} %copy-done.6, s32[324,1024]{1,0:T(8,128)S(1)} %copy-done.1, s32[324,1024]{1,0:T(8,128)S(1)} %copy-done.2), custom_call_target="tpu_custom_call" | custom-call | flops 16588800 | bytes 3981312 | tf_op jit(solution)/shard_map/pallas_call | solution.py:391
  15.3 0.0 copy-start.4
  15.3 0.0 copy-start.5
  15.4 3.9 %all-to-all-done = bf16[32,24,128]{2,1,0:T(8,128)(2,1)S(1)} async-done(((bf16[32,24,128]{2,1,0:T(8,128)(2,1)}), bf16[32,24,128]{2,1,0:T(8,128)(2,1)S(1)}, u32[]{:S(2)}, u32[]{:S(2)}) %all-to-all-start) | async-done | bytes 196640 | tf_op jit(solution)/shard_map/all_to_all | solution.py:382
  19.2 48.6 %shard_map.84 = f32[32,2,8,128]{3,2,1,0:T(8,128)} custom-call(s32[16]{0:T(128)S(1)} %copy-done.6, s32[1]{0:T(128)} %constant.29.clone.1.part_ref, bf16[768,128]{1,0:T(8,128)(2,1)S(1)} %bitcast.4, bf16[384,384]{1,0:T(8,128)(2,1)S(1)} %pad.4.integ_ref, s32[8,336,128]{2,1,0:T(8,128)S(1)} %shard_map.83.spot_ref), custom_call_target="tpu_custom_call" | custom-call | tf_op jit(solution)/shard_map/pallas_call | solution.py:404
  67.8 2.7 %all-to-all-start.1 = ((f32[32,2,8,128]{3,2,1,0:T(8,128)}), f32[32,2,8,128]{3,2,1,0:T(8,128)S(1)}, u32[]{:S(2)}, u32[]{:S(2)}) async-start(f32[32,2,8,128]{3,2,1,0:T(8,128)} %shard_map.84), calls=%async_computation.1 | async-start | bytes 524288 | tf_op jit(solution)/shard_map/all_to_all | solution.py:425
  70.6 0.1 dynamic_slice.9.irrep_ref
  70.7 10.3 %all-to-all-done.1 = f32[32,2,8,128]{3,2,1,0:T(8,128)S(1)} async-done(((f32[32,2,8,128]{3,2,1,0:T(8,128)}), f32[32,2,8,128]{3,2,1,0:T(8,128)S(1)}, u32[]{:S(2)}, u32[]{:S(2)}) %all-to-all-start.1) | async-done | bytes 262176 | tf_op jit(solution)/shard_map/all_to_all | solution.py:425
  81.0 0.0 copy-done.4
  81.0 0.0 copy-done.5
  81.0 1.4 %shard_map.85 = f32[256,256]{1,0:T(8,128)} custom-call(s32[4]{0:T(128)S(1)} %dynamic_slice.9.irrep_ref, f32[512,128]{1,0:T(8,128)S(1)} %bitcast.3, f32[256,256]{1,0:T(8,128)S(1)} %copy-done.5, bf16[256,256]{1,0:T(8,128)(2,1)S(1)} %copy-done.4), custom_call_target="tpu_custom_call" | custom-call | tf_op jit(solution)/shard_map/pallas_call | solution.py:427
Async XLA Ops:
  0.0 1.0 %copy-start = (s32[4,20736]{1,0:T(4,128)S(1)}, s32[4,20736]{1,0:T(4,128)}, u32[]{:S(2)}) copy-start(s32[4,20736]{1,0:T(4,128)} %param.14) | copy-start | bytes 995332
  0.0 11.5 %copy-start.1 = (s32[324,1024]{1,0:T(8,128)S(1)}, s32[324,1024]{1,0:T(8,128)}, u32[]{:S(2)}) copy-start(s32[324,1024]{1,0:T(8,128)} %row_ref.1) | copy-start | bytes 3981316
  1.4 0.9 %copy-start.3 = (bf16[256,256]{1,0:T(8,128)(2,1)S(1)}, bf16[256,256]{1,0:T(8,128)(2,1)}, u32[]{:S(2)}) copy-start(bf16[256,256]{1,0:T(8,128)(2,1)} %coef_ref.3) | copy-start | bytes 393220
  2.3 9.1 %copy-start.6 = (s32[16]{0:T(128)S(1)}, s32[16]{0:T(128)}, u32[]{:S(2)}) copy-start(s32[16]{0:T(128)} %irrep_ref.3) | copy-start | bytes 196
  3.2 16.1 %all-to-all-start = ((bf16[32,24,128]{2,1,0:T(8,128)(2,1)}), bf16[32,24,128]{2,1,0:T(8,128)(2,1)S(1)}, u32[]{:S(2)}, u32[]{:S(2)}) async-start(bf16[32,24,128]{2,1,0:T(8,128)(2,1)} %bitcast), calls=%async_computation | async-start | bytes 393216 | tf_op jit(solution)/shard_map/all_to_all | solution.py:382
  11.5 1.3 %copy-start.2 = (s32[324,1024]{1,0:T(8,128)S(1)}, s32[324,1024]{1,0:T(8,128)}, u32[]{:S(2)}) copy-start(s32[324,1024]{1,0:T(8,128)} %sign_ref.1) | copy-start | bytes 3981316
  15.3 65.6 %copy-start.4 = (bf16[256,256]{1,0:T(8,128)(2,1)S(1)}, bf16[256,256]{1,0:T(8,128)(2,1)}, u32[]{:S(2)}) copy-start(bf16[256,256]{1,0:T(8,128)(2,1)} %coef_ref.3) | copy-start | bytes 393220
  15.3 65.6 %copy-start.5 = (f32[256,256]{1,0:T(8,128)S(1)}, f32[256,256]{1,0:T(8,128)}, u32[]{:S(2)}) copy-start(f32[256,256]{1,0:T(8,128)} %diag_ref.1) | copy-start | bytes 786436
  67.8 13.1 %all-to-all-start.1 = ((f32[32,2,8,128]{3,2,1,0:T(8,128)}), f32[32,2,8,128]{3,2,1,0:T(8,128)S(1)}, u32[]{:S(2)}, u32[]{:S(2)}) async-start(f32[32,2,8,128]{3,2,1,0:T(8,128)} %shard_map.84), calls=%async_computation.1 | async-start | bytes 524288 | tf_op jit(solution)/shard_map/all_to_all | solution.py:425
where the time goes:
time: 82.7 us; the launch traced here: 82.3 us
  Pallas kernels  53.3 us (64%)
  waiting for transfers between devices  14.2 us (17%)
  starting transfers between devices  10 us (12%)
  local copies, waits for them, and re-layouts  3.76 us (5%)
  other arithmetic  0.94 us (1%)
    pallas_call x1, Pallas kernels, on_device(): pl.pallas_call(functools.partial(main_kernel, z), out_shape=jax.ShapeDtyp...  48.6 us
    all_to_all x1, waiting for transfers between devices, on_device(): lax.all_to_all(terms, ('alpha', 'beta'), 0, 0, tiled=True)  10.3 us
    all_to_all x1, starting transfers between devices, on_device(): lax.all_to_all(packed.reshape(z.devices, z.pack, LANES), ('alpha', 'beta'...  7.3 us
    all_to_all x1, waiting for transfers between devices, on_device(): lax.all_to_all(packed.reshape(z.devices, z.pack, LANES), ('alpha', 'beta'...  3.88 us
    all_to_all x1, starting transfers between devices, on_device(): lax.all_to_all(terms, ('alpha', 'beta'), 0, 0, tiled=True)  2.72 us
    pallas_call x1, Pallas kernels, on_device(): pl.pallas_call(functools.partial(index_kernel, z), out_shape=jax.ShapeDty...  2.5 us
    unnamed x14, local copies, waits for them, and re-layouts  2.38 us
  transfers between devices with their start and end apart: 2, of which 2 were waited for; matrix products, arithmetic and copies ran while one was open for 1% of the time, Pallas kernels for 3%

commit v1 on v0

--- a/solution.py
+++ b/solution.py
@@ -9,8 +9,8 @@
 
 LANES = 128
 DEPTH = 512
-SPAN = 256
-GATHERED = 4
+WIDE = 256
+GATHERED = 3
 VMEM = pl.BlockSpec(memory_space=pltpu.VMEM)
 SMEM = pl.BlockSpec(memory_space=pltpu.SMEM)
 
@@ -80,6 +80,8 @@
     count = jnp.int32(0)
     lane_row = lax.broadcasted_iota(jnp.int32, (1, LANES), 1)
     ranks = jnp.full((1, LANES), -1, jnp.int32)
+    for extra in range(z.blocks + 8):
+        list_ref[extra] = 0
     for g in range(z.blocks):
         live = irrep_ref[g] == 0
         rank = jnp.where(live, count, -1)
@@ -200,7 +202,6 @@
     lax.fori_loop(0, z.targets // step, weight_step, 0, unroll=2)
 
     lane_list = lax.broadcasted_iota(jnp.int32, (z.lists, LANES), 1)
-    chunk_tiles = SPAN // LANES
 
     def compact_step(u, carry):
         first, second = list_ref[2 * u], list_ref[2 * u + 1]
@@ -210,24 +211,37 @@
         right = pltpu.roll(full[second // 2], right_shift, 1)
         left = jnp.where(2 * u < count, left, 0.0)
         right = jnp.where(2 * u + 1 < count, right, 0.0)
-        at_list = pl.ds(pl.multiple_of(u // chunk_tiles * z.lists, z.lists), z.lists)
-        at_lane = pl.ds(pl.multiple_of(u % chunk_tiles * LANES, LANES), LANES)
-        both = jnp.where(lane_list < half_block, left, right)
-        tabf[u] = both
-        table[at_list, at_lane] = both.astype(bf16)
+        tabf[u] = jnp.where(lane_list < half_block, left, right)
         return carry
 
-    lax.fori_loop(0, (n_tiles + chunk_tiles - 1) // chunk_tiles * chunk_tiles, compact_step, 0)
-
-    local = lax.broadcasted_iota(jnp.int32, (SPAN, LANES), 0).astype(f32).astype(bf16)
-    nothing = jnp.zeros((SPAN, LANES), bf16)
+    lax.fori_loop(0, z.tiles, compact_step, 0)
+
     side = 2 * z.targets
 
-    def tall_row(few):
-        return jnp.concatenate([few.astype(f32).astype(bf16)] * (SPAN // 16), axis=0)
-
-    def run(tiles):
-        depth = (tiles * LANES + SPAN - 1) // SPAN
+    def run(blocks, span):
+        depth = (blocks * z.block + span - 1) // span
+        tiles = (blocks + 1) // 2
+        local = lax.broadcasted_iota(jnp.int32, (span, LANES), 0).astype(f32).astype(bf16)
+        nothing = jnp.zeros((span, LANES), bf16)
+
+        def tall_row(few):
+            return jnp.concatenate([few.astype(f32).astype(bf16)] * (span // 16), axis=0)
+
+        def chunk_of(spot):
+            if span & (span - 1) == 0:
+                return lax.shift_right_arithmetic(spot, span.bit_length() - 1)
+            return sum((spot >= span * m).astype(jnp.int32) for m in range(1, depth))
+
+        for m in range(depth):
+            for k in range(0, span, LANES):
+                block = (m * span + k) // z.block
+                left, right = tabf[min(block // 2, z.tiles - 1)], jnp.zeros((z.lists, LANES), f32)
+                if block % 2:
+                    left = pltpu.roll(left, half_block, 1)
+                    if block // 2 + 1 < z.tiles:
+                        right = pltpu.roll(tabf[block // 2 + 1], half_block, 1)
+                    left = jnp.where(lane_list < half_block, left, right)
+                table[m * z.lists : (m + 1) * z.lists, k : k + LANES] = left.astype(bf16)
 
         def one_tile(u, carry, turn=False):
             acc[...] = jnp.zeros_like(acc)
@@ -280,12 +294,13 @@
                         gather(q, spot[0:8], sign[0:8].astype(f32))
                         continue
                     chosen.append(q)
-                    hit = local == tall_row(spot & (SPAN - 1))
+                    part = chunk_of(spot)
+                    hit = local == tall_row(spot - part * span)
                     picks.append(jnp.where(hit, tall_row(sign), nothing))
-                    chunk.append(lax.shift_right_arithmetic(spot[0:8], SPAN.bit_length() - 1))
+                    chunk.append(part[0:8])
                 pick = jnp.concatenate(picks, axis=1)
                 found = jnp.dot(
-                    table[0 : depth * z.lists, :], pick, preferred_element_type=f32
+                    table[0 : depth * z.lists, 0:span], pick, preferred_element_type=f32
                 )
                 for k, q in enumerate(chosen):
                     lanes = slice(k * LANES, (k + 1) * LANES)
@@ -313,9 +328,11 @@
             lax.fori_loop(0, mine, lambda n, carry: one_tile(n * z.share + part, carry, True), 0)
 
     lower = 0
-    for tiles in sorted({min(tiles, z.tiles) for tiles in (4, 5, 6, 8, z.tiles)}):
-        pl.when((n_tiles > lower) & (n_tiles <= tiles))(functools.partial(run, tiles))
-        lower = tiles
+    cases = [(6, 192), (8, WIDE), (9, 192), (10, WIDE), (12, WIDE), (16, WIDE), (z.blocks, WIDE)]
+    for blocks, span in cases:
+        if lower < blocks <= z.blocks:
+            pl.when((count > lower) & (count <= blocks))(functools.partial(run, blocks, span))
+            lower = blocks
 
     wide = z.src * z.strings
     lane_out = lax.broadcasted_iota(jnp.int32, (z.targets * z.strings, LANES), 1)
@@ -410,7 +427,7 @@
             pltpu.VMEM((z.devices * z.pack, LANES), f32),
             pltpu.VMEM((z.tiles, z.lists, LANES), f32),
             pltpu.VMEM((z.tiles, z.lists, LANES), f32),
-            pltpu.VMEM((z.tiles * LANES // SPAN * z.lists, SPAN), bf16),
+            pltpu.VMEM((round_up(z.all_rows, WIDE) // WIDE * z.lists, WIDE), bf16),
             pltpu.VMEM((z.pair_tiles, z.lists, LANES), f32),
             pltpu.VMEM((z.pair_rows * z.targets, LANES), f32),
             pltpu.VMEM((z.chunks, LANES, DEPTH), bf16),

time: 82.7 us -> 83.4 us (level)
  no operation moved by 1% of the time
where the time goes in v1:
time: 83.4 us; the launch traced here: 83.1 us
  Pallas kernels  54.1 us (65%)
  waiting for transfers between devices  14.2 us (17%)
  starting transfers between devices  9.98 us (12%)
  local copies, waits for them, and re-layouts  3.76 us (5%)
  other arithmetic  0.94 us (1%)
    pallas_call x1, Pallas kernels, on_device(): pl.pallas_call(functools.partial(main_kernel, z), out_shape=jax.ShapeDtyp...  49.4 us
    all_to_all x1, waiting for transfers between devices, on_device(): lax.all_to_all(terms, ('alpha', 'beta'), 0, 0, tiled=True)  10.3 us
    all_to_all x1, starting transfers between devices, on_device(): lax.all_to_all(packed.reshape(z.devices, z.pack, LANES), ('alpha', 'beta'...  7.3 us
    all_to_all x1, waiting for transfers between devices, on_device(): lax.all_to_all(packed.reshape(z.devices, z.pack, LANES), ('alpha', 'beta'...  3.88 us
    all_to_all x1, starting transfers between devices, on_device(): lax.all_to_all(terms, ('alpha', 'beta'), 0, 0, tiled=True)  2.68 us
    pallas_call x1, Pallas kernels, on_device(): pl.pallas_call(functools.partial(index_kernel, z), out_shape=jax.ShapeDty...  2.51 us
    unnamed x14, local copies, waits for them, and re-layouts  2.38 us
  transfers between devices with their start and end apart: 2, of which 2 were waited for; matrix products, arithmetic and copies ran while one was open for 1% of the time, Pallas kernels for 3%

profile of v1, /device:TPU:0, one launch (start us, length us, event | category | flops | bytes accessed | tf_op | source)
XLA Modules:
  0.0 83.1 jit_solution(10168267760002874921)
XLA Ops:
  0.0 0.0 copy-start
  0.0 0.0 copy-start.1
  0.0 0.8 %add_reduce_fusion = s32[324]{0:T(512)S(1)} fusion(s32[4,324]{1,0:T(4,128)} %param.13, s32[]{:T(128)S(6)} %select_n.13), kind=kLoop, calls=%fused_computation.2 | loop fusion | flops 324 | bytes 2596 | tf_op jit(solution)/shard_map/add | solution.py:390
  0.8 0.1 copy-done
  1.0 0.2 dynamic-slice_reduce_fusion
  1.2 0.1 reshape.55
  1.3 0.1 multiply_convert_fusion.sign_ref
  1.4 0.0 copy-start.3
  1.4 0.9 %copy-done.3 = bf16[256,256]{1,0:T(8,128)(2,1)S(1)} copy-done((bf16[256,256]{1,0:T(8,128)(2,1)S(1)}, bf16[256,256]{1,0:T(8,128)(2,1)}, u32[]{:S(2)}) %copy-start.3) | copy-done | bytes 131096
  2.3 0.0 copy-start.6
  2.3 0.8 %shard_map.82 = bf16[768,128]{1,0:T(8,128)(2,1)} custom-call(bf16[256,256]{1,0:T(8,128)(2,1)S(1)} %copy-done.3, f32[1,324,64]{2,1,0:T(8,128)S(1)} %multiply_convert_fusion.sign_ref), custom_call_target="tpu_custom_call" | custom-call | tf_op jit(solution)/shard_map/pallas_call | solution.py:391
  3.2 7.3 %all-to-all-start = ((bf16[32,24,128]{2,1,0:T(8,128)(2,1)}), bf16[32,24,128]{2,1,0:T(8,128)(2,1)S(1)}, u32[]{:S(2)}, u32[]{:S(2)}) async-start(bf16[32,24,128]{2,1,0:T(8,128)(2,1)} %bitcast), calls=%async_computation | async-start | bytes 393216 | tf_op jit(solution)/shard_map/all_to_all | solution.py:399
  10.5 1.0 %pad.4.integ_ref = bf16[384,384]{1,0:T(8,128)(2,1)S(1)} pad(bf16[324,324]{1,0:T(8,128)(2,1)} %param.10, bf16[]{:T(256)} %constant.32.clone.1), padding=0_60x0_60 | pad | bytes 504866 | tf_op jit(solution)/shard_map/jit(_pad)/pad | solution.py:406
  11.5 0.0 copy-done.1
  11.5 0.0 copy-done.6
  11.5 0.0 copy-start.2
  11.5 1.3 %copy-done.2 = s32[324,1024]{1,0:T(8,128)S(1)} copy-done((s32[324,1024]{1,0:T(8,128)S(1)}, s32[324,1024]{1,0:T(8,128)}, u32[]{:S(2)}) %copy-start.2) | copy-done | bytes 1327128
  12.8 2.5 %shard_map.83.spot_ref = s32[8,336,128]{2,1,0:T(8,128)S(1)} custom-call(s32[16]{0:T(128)S(1)} %copy-done.6, s32[324,1024]{1,0:T(8,128)S(1)} %copy-done.1, s32[324,1024]{1,0:T(8,128)S(1)} %copy-done.2), custom_call_target="tpu_custom_call" | custom-call | flops 16588800 | bytes 3981312 | tf_op jit(solution)/shard_map/pallas_call | solution.py:408
  15.3 0.0 copy-start.4
  15.3 0.0 copy-start.5
  15.4 3.9 %all-to-all-done = bf16[32,24,128]{2,1,0:T(8,128)(2,1)S(1)} async-done(((bf16[32,24,128]{2,1,0:T(8,128)(2,1)}), bf16[32,24,128]{2,1,0:T(8,128)(2,1)S(1)}, u32[]{:S(2)}, u32[]{:S(2)}) %all-to-all-start) | async-done | bytes 196640 | tf_op jit(solution)/shard_map/all_to_all | solution.py:399
  19.2 49.4 %shard_map.84 = f32[32,2,8,128]{3,2,1,0:T(8,128)} custom-call(s32[16]{0:T(128)S(1)} %copy-done.6, s32[1]{0:T(128)} %constant.29.clone.1.part_ref, bf16[768,128]{1,0:T(8,128)(2,1)S(1)} %bitcast.4, bf16[384,384]{1,0:T(8,128)(2,1)S(1)} %pad.4.integ_ref, s32[8,336,128]{2,1,0:T(8,128)S(1)} %shard_map.83.spot_ref), custom_call_target="tpu_custom_call" | custom-call | tf_op jit(solution)/shard_map/pallas_call | solution.py:421
  68.6 2.7 %all-to-all-start.1 = ((f32[32,2,8,128]{3,2,1,0:T(8,128)}), f32[32,2,8,128]{3,2,1,0:T(8,128)S(1)}, u32[]{:S(2)}, u32[]{:S(2)}) async-start(f32[32,2,8,128]{3,2,1,0:T(8,128)} %shard_map.84), calls=%async_computation.1 | async-start | bytes 524288 | tf_op jit(solution)/shard_map/all_to_all | solution.py:442
  71.3 0.1 dynamic_slice.9.irrep_ref
  71.4 10.3 %all-to-all-done.1 = f32[32,2,8,128]{3,2,1,0:T(8,128)S(1)} async-done(((f32[32,2,8,128]{3,2,1,0:T(8,128)}), f32[32,2,8,128]{3,2,1,0:T(8,128)S(1)}, u32[]{:S(2)}, u32[]{:S(2)}) %all-to-all-start.1) | async-done | bytes 262176 | tf_op jit(solution)/shard_map/all_to_all | solution.py:442
  81.7 0.0 copy-done.4
  81.7 0.0 copy-done.5
  81.7 1.4 %shard_map.85 = f32[256,256]{1,0:T(8,128)} custom-call(s32[4]{0:T(128)S(1)} %dynamic_slice.9.irrep_ref, f32[512,128]{1,0:T(8,128)S(1)} %bitcast.3, f32[256,256]{1,0:T(8,128)S(1)} %copy-done.5, bf16[256,256]{1,0:T(8,128)(2,1)S(1)} %copy-done.4), custom_call_target="tpu_custom_call" | custom-call | tf_op jit(solution)/shard_map/pallas_call | solution.py:444
Async XLA Ops:
  0.0 1.0 %copy-start = (s32[4,20736]{1,0:T(4,128)S(1)}, s32[4,20736]{1,0:T(4,128)}, u32[]{:S(2)}) copy-start(s32[4,20736]{1,0:T(4,128)} %param.14) | copy-start | bytes 995332
  0.0 11.5 %copy-start.1 = (s32[324,1024]{1,0:T(8,128)S(1)}, s32[324,1024]{1,0:T(8,128)}, u32[]{:S(2)}) copy-start(s32[324,1024]{1,0:T(8,128)} %row_ref.1) | copy-start | bytes 3981316
  1.4 0.9 %copy-start.3 = (bf16[256,256]{1,0:T(8,128)(2,1)S(1)}, bf16[256,256]{1,0:T(8,128)(2,1)}, u32[]{:S(2)}) copy-start(bf16[256,256]{1,0:T(8,128)(2,1)} %coef_ref.3) | copy-start | bytes 393220
  2.3 9.1 %copy-start.6 = (s32[16]{0:T(128)S(1)}, s32[16]{0:T(128)}, u32[]{:S(2)}) copy-start(s32[16]{0:T(128)} %irrep_ref.3) | copy-start | bytes 196
  3.2 16.1 %all-to-all-start = ((bf16[32,24,128]{2,1,0:T(8,128)(2,1)}), bf16[32,24,128]{2,1,0:T(8,128)(2,1)S(1)}, u32[]{:S(2)}, u32[]{:S(2)}) async-start(bf16[32,24,128]{2,1,0:T(8,128)(2,1)} %bitcast), calls=%async_computation | async-start | bytes 393216 | tf_op jit(solution)/shard_map/all_to_all | solution.py:399
  11.5 1.3 %copy-start.2 = (s32[324,1024]{1,0:T(8,128)S(1)}, s32[324,1024]{1,0:T(8,128)}, u32[]{:S(2)}) copy-start(s32[324,1024]{1,0:T(8,128)} %sign_ref.1) | copy-start | bytes 3981316
  15.3 66.3 %copy-start.4 = (bf16[256,256]{1,0:T(8,128)(2,1)S(1)}, bf16[256,256]{1,0:T(8,128)(2,1)}, u32[]{:S(2)}) copy-start(bf16[256,256]{1,0:T(8,128)(2,1)} %coef_ref.3) | copy-start | bytes 393220
  15.3 66.3 %copy-start.5 = (f32[256,256]{1,0:T(8,128)S(1)}, f32[256,256]{1,0:T(8,128)}, u32[]{:S(2)}) copy-start(f32[256,256]{1,0:T(8,128)} %diag_ref.1) | copy-start | bytes 786436
  68.6 13.1 %all-to-all-start.1 = ((f32[32,2,8,128]{3,2,1,0:T(8,128)}), f32[32,2,8,128]{3,2,1,0:T(8,128)S(1)}, u32[]{:S(2)}, u32[]{:S(2)}) async-start(f32[32,2,8,128]{3,2,1,0:T(8,128)} %shard_map.84), calls=%async_computation.1 | async-start | bytes 524288 | tf_op jit(solution)/shard_map/all_to_all | solution.py:442
